TPU v7x, 32 devices: a whole 2x2x4 slice. The times are simulated.
32 devices in a mesh: row: 4 (over y, x), col: 8 (over z, core).
Axes of the slice: x: 2, y: 2, z: 4, core: 2. Of those that a mesh axis runs over, the one named last changes fastest.
Arguments:
- galaxy: float32 [128, 256, 256], P('row', 'col'), may hold values from 0.03 to 32, as said below
- randoms: float32 [128, 256, 256], P('row', 'col'), may hold values from 0.5 to 4
- coverage: int32 [128, 256, 256], P('row', 'col'), may hold values from 0 to 1
- patch: int32 [128, 256, 256], P('row', 'col'), may hold values from 0 to 127
Outputs:
- contrast: float32 [128, 256, 256], P('row', 'col')
- patch_sums: float32 [4, 128], replicated
Inputs may be any that keep to these rules, and one draw needn't show every extreme that they name: `galaxy`: positive densities.
All inputs are finite; a program needn't handle non-finite values.
Results may differ from a plain program's by a relative error of at most 0.00016.
Values sent between devices are 32-bit elements; how exact they have to be, the bound alone decides.
A program may use at most 64 MiB of HBM per device.

v0:
```python
import jax
import jax.numpy as jnp
from jax import lax
from jax.sharding import PartitionSpec as P

RADIUS = 16
NPATCH = 128


def extended_2(array, sides, width):
    for axis, dim in sides:
        devices, length = (lax.axis_size(axis), array.shape[dim])
        up = [(i, (i + 1) % devices) for i in range(devices - 1)]
        down = [(j, i) for i, j in up]
        last = lax.slice_in_dim(array, length - width, length, axis=dim)
        first = lax.slice_in_dim(array, 0, width, axis=dim)
        before = lax.ppermute(last, axis, up)
        after = lax.ppermute(first, axis, down)
        array = jnp.concatenate([before, array, after], axis=dim)
    return array


def kernel_taps(radius):
    offs = jnp.arange(-radius, radius + 1).astype(jnp.float32)
    sigma = radius / 2.0
    vals = jnp.exp(-offs * offs / (2.0 * sigma * sigma))
    return vals / jnp.sum(vals)


def valid_taps(padded, taps, radius, axis):
    count = padded.shape[axis] - 2 * radius
    total = lax.slice_in_dim(padded, 0, count, axis=axis) * taps[0]
    for j in range(1, 2 * radius + 1):
        total = total + taps[j] * lax.slice_in_dim(padded, j, j + count, axis=axis)
    return total


def local(galaxy, randoms, coverage, patch):
    radius = RADIUS
    taps = kernel_taps(radius)
    fields = jnp.stack([galaxy, randoms])
    widths = ((0, 0), (0, 0), (0, 0), (radius, radius))
    zsmooth = valid_taps(jnp.pad(fields, widths), taps, radius, 3)
    cover = coverage.astype(jnp.float32)
    totals = lax.psum((jnp.sum(cover * galaxy), jnp.sum(cover * randoms)), ("row", "col"))
    extended = extended_2(zsmooth, (("row", 1), ("col", 2)), radius)
    xsmooth = valid_taps(extended, taps, radius, 1)
    smoothed = valid_taps(xsmooth, taps, radius, 2)
    alpha = totals[0] / totals[1]
    nbar = alpha * smoothed[1]
    weight = 1.0 / (1.0 + 2.0 * nbar)
    contrast = cover * weight * (smoothed[0] / nbar - 1.0)
    rows_x, rows_y, depth = contrast.shape
    per_row = rows_y * depth
    block = 1
    for cand in range(1, rows_x + 1):
        if rows_x % cand == 0 and cand * per_row <= 32768:
            block = cand
    steps_count = rows_x // block
    flat_c = contrast.reshape(steps_count, block * per_row)
    flat_m = cover.reshape(steps_count, block * per_row)
    flat_p = patch.reshape(steps_count, block * per_row)
    labels = jnp.arange(NPATCH, dtype=jnp.int32)

    def accumulate(carry, items):
        cvals, mvals, pvals = items
        powers = jnp.stack(
            [mvals, mvals * cvals, mvals * cvals * cvals, mvals * cvals * cvals * cvals]
        )
        onehot = (pvals[None, :] == labels[:, None]).astype(jnp.float32)
        part_sums = lax.dot_general(
            powers,
            onehot,
            (((1,), (1,)), ((), ())),
            precision=lax.Precision.HIGHEST,
            preferred_element_type=jnp.float32,
        )
        return (carry + part_sums, None)

    local_sums, unused = lax.scan(
        accumulate, jnp.zeros((4, NPATCH), jnp.float32), (flat_c, flat_m, flat_p)
    )
    whole_sums = lax.psum(local_sums, ("row", "col"))
    scale = NPATCH / (rows_x * lax.axis_size("row") * rows_y * lax.axis_size("col") * depth)
    return (contrast, whole_sums * scale)


def solution(mesh):
    in_specs = (
        P("row", "col", None),
        P("row", "col", None),
        P("row", "col", None),
        P("row", "col", None),
    )
    out_specs = (P("row", "col", None), P())
    return jax.shard_map(local, mesh=mesh, in_specs=in_specs, out_specs=out_specs, check_vma=False)
```

profile of v0, /device:TPU:0, one launch (start us, length us, event | category | flops | bytes accessed | tf_op | source)
XLA Modules:
  0.0 384.6 jit_solution(8935265958357768094)
XLA Ops:
  3.4 3.1 pad_maximum_fusion.2
  6.5 64.2 %fusion.99 = f32[2,32,32,256]{3,2,1,0:T(8,128)S(1)} fusion(f32[2,32,32,256]{3,2,1,0:T(8,128)} %pad_maximum_fusion.2, f32[]{:T(128)} %bitcast.34, f32[]{:T(128)} %bitcast.33, f32[]{:T(128)} %bitcast.32, f32[]{:T(128)} %bitcast.31, f32[]{:T(128)} %bitcast.30, f32[]{:T(128)} %bitcast.29, f32[]{:T(128)} %bitcast.28, f32[]{:T(128)} %bitcast.27, f32[]{:T(128)} %bitcast.26, ...), kind=kLoop, calls=%fused_computation.171 | loop fusion | flops 34078720 | bytes 4194436 | tf_op jit(solution)/shard_map/add | solution.py:34
  70.9 4.9 %collective-permute-start = (f32[2,16,32,256]{3,2,1,0:T(8,128)S(1)}, f32[2,16,32,256]{3,2,1,0:T(8,128)S(1)}, u32[]{:S(2)}, u32[]{:S(2)}) collective-permute-start(f32[2,16,32,256]{3,2,1,0:T(8,128)S(1)} %get-tuple-element.75), channel_id=1, source_target_pairs={{0,8},{8,16},{16,24},{1,9},{9,17},{17,25},{2,10},{10,18},{18,26},{... | collective-permute-start | bytes 3145736 | tf_op jit(solution)/shard_map/ppermute | solution.py:17
  77.2 21.0 %collective-permute-done = f32[2,16,32,256]{3,2,1,0:T(8,128)S(1)} collective-permute-done((f32[2,16,32,256]{3,2,1,0:T(8,128)S(1)}, f32[2,16,32,256]{3,2,1,0:T(8,128)S(1)}, u32[]{:S(2)}, u32[]{:S(2)}) %collective-permute-start) | collective-permute-done | bytes 1048608 | tf_op jit(solution)/shard_map/ppermute | solution.py:17
  98.2 24.4 %collective-permute-done.1 = f32[2,16,32,256]{3,2,1,0:T(8,128)S(1)} collective-permute-done((f32[2,16,32,256]{3,2,1,0:T(8,128)S(1)}, f32[2,16,32,256]{3,2,1,0:T(8,128)S(1)}, u32[]{:S(2)}, u32[]{:S(2)}) %collective-permute-start.1) | collective-permute-done | bytes 1048608 | tf_op jit(solution)/shard_map/ppermute | solution.py:18
  123.7 2.4 fusion.147
  126.1 2.6 collective-permute-start.2
  131.1 46.6 %all-reduce.1 = (f32[]{:T(128)}, f32[]{:T(128)}) all-reduce(f32[]{:T(128)} %get-tuple-element.56, f32[]{:T(128)} %get-tuple-element.55), channel_id=1, replica_groups=mesh['row'=4,'col'=8] {'row','col'}, use_global_device_ids=true, to_apply=%region_1.2 | all-reduce | flops 2 | bytes 16 | tf_op jit(solution)/shard_map/psum | solution.py:45
  178.8 2.5 reshape.25
  181.3 2.4 reshape.27
  185.0 3.3 pad_maximum_fusion
  188.3 36.4 %fusion.13 = f32[2,32,64,256]{3,2,1,0:T(8,128)S(1)} fusion(f32[2,64,64,256]{3,2,1,0:T(8,128)S(1)} %pad_maximum_fusion, f32[]{:T(128)} %bitcast.34, f32[]{:T(128)} %bitcast.33, f32[]{:T(128)} %bitcast.32, f32[]{:T(128)} %bitcast.31, f32[]{:T(128)} %bitcast.30, f32[]{:T(128)} %bitcast.29, f32[]{:T(128)} %bitcast.28, f32[]{:T(128)} %bitcast.27, f32[]{:T(128)} %bitcast.26, ...), kind=kLoop, calls=%fused_computation.52 | loop fusion | flops 68157440 | bytes 142606464 | tf_op jit(solution)/shard_map/add | solution.py:34
  224.8 28.9 %fusion.109 = f32[2,32,32,256]{3,2,1,0:T(8,128)S(1)} fusion(f32[2,32,64,256]{3,2,1,0:T(8,128)S(1)} %fusion.13, f32[]{:T(128)} %bitcast.34, f32[]{:T(128)} %bitcast.33, f32[]{:T(128)} %bitcast.32, f32[]{:T(128)} %bitcast.31, f32[]{:T(128)} %bitcast.30, f32[]{:T(128)} %bitcast.29, f32[]{:T(128)} %bitcast.28, f32[]{:T(128)} %bitcast.27, f32[]{:T(128)} %bitcast.26, ...), kind=kLoop, calls=%fused_computation.182 | loop fusion | flops 34078720 | bytes 71303296 | tf_op jit(solution)/shard_map/add | solution.py:34
  255.0 87.6 %while.11 = (s32[]{:T(128)}, f32[4,128]{1,0:T(4,128)S(1)}, f32[8,32768]{1,0:T(8,128)}, f32[8,32768]{1,0:T(8,128)S(1)}, s32[8,32768]{1,0:T(8,128)}, /*index=5*/s32[]{:T(128)}, s32[]{:T(128)}) while((s32[]{:T(128)}, f32[4,128]{1,0:T(4,128)S(1)}, f32[8,32768]{1,0:T(8,128)}, f32[8,32768]{1,0:T(8,128)S(1)}, s32[8,32768]{1,0:T(8,128)}, ...), condition=%wide.region_6.7_spmd.clone, body=%wide.region_5.6_spmd.clone.sunk | while | flops 206013440 | bytes 1708127 | solution.py:80
  255.0 1.5 dynamic-slice_multiply_fusion.6
  256.5 1.3 constant_dynamic-slice_fusion.3
  257.8 8.1 %fusion.154 = f32[4,128]{1,0:T(4,128)S(1)} fusion(s32[32768]{0:T(1024)S(1)} %bitcast.48, f32[1,32768]{1,0:T(1,128)S(1)} %get-tuple-element.145, f32[1,32768]{1,0:T(1,128)S(1)} %get-tuple-element.146, f32[1,32768]{1,0:T(1,128)S(1)} %get-tuple-element.147, f32[1,32768]{1,0:T(1,128)S(1)} %get-tuple-element.148, f32[4,128]{1,0:T(4,128)S(1)} %get-tuple-element.157, ...), kind=kOutput, calls=%fused_computation.4.clone.1 | convolution fusion | flops 205915136 | bytes 659457 | tf_op jit(solution)/shard_map/while/body/eval_jaxpr/dot_general | solution.py:71
  265.9 1.5 dynamic-slice_multiply_fusion.6
  268.8 8.1 %fusion.154 = f32[4,128]{1,0:T(4,128)S(1)} fusion(s32[32768]{0:T(1024)S(1)} %bitcast.48, f32[1,32768]{1,0:T(1,128)S(1)} %get-tuple-element.145, f32[1,32768]{1,0:T(1,128)S(1)} %get-tuple-element.146, f32[1,32768]{1,0:T(1,128)S(1)} %get-tuple-element.147, f32[1,32768]{1,0:T(1,128)S(1)} %get-tuple-element.148, f32[4,128]{1,0:T(4,128)S(1)} %get-tuple-element.157, ...), kind=kOutput, calls=%fused_computation.4.clone.1 | convolution fusion | flops 205915136 | bytes 659457 | tf_op jit(solution)/shard_map/while/body/eval_jaxpr/dot_general | solution.py:71
  276.9 1.5 dynamic-slice_multiply_fusion.6
  279.7 8.1 %fusion.154 = f32[4,128]{1,0:T(4,128)S(1)} fusion(s32[32768]{0:T(1024)S(1)} %bitcast.48, f32[1,32768]{1,0:T(1,128)S(1)} %get-tuple-element.145, f32[1,32768]{1,0:T(1,128)S(1)} %get-tuple-element.146, f32[1,32768]{1,0:T(1,128)S(1)} %get-tuple-element.147, f32[1,32768]{1,0:T(1,128)S(1)} %get-tuple-element.148, f32[4,128]{1,0:T(4,128)S(1)} %get-tuple-element.157, ...), kind=kOutput, calls=%fused_computation.4.clone.1 | convolution fusion | flops 205915136 | bytes 659457 | tf_op jit(solution)/shard_map/while/body/eval_jaxpr/dot_general | solution.py:71
  287.9 1.5 dynamic-slice_multiply_fusion.6
  290.7 8.1 %fusion.154 = f32[4,128]{1,0:T(4,128)S(1)} fusion(s32[32768]{0:T(1024)S(1)} %bitcast.48, f32[1,32768]{1,0:T(1,128)S(1)} %get-tuple-element.145, f32[1,32768]{1,0:T(1,128)S(1)} %get-tuple-element.146, f32[1,32768]{1,0:T(1,128)S(1)} %get-tuple-element.147, f32[1,32768]{1,0:T(1,128)S(1)} %get-tuple-element.148, f32[4,128]{1,0:T(4,128)S(1)} %get-tuple-element.157, ...), kind=kOutput, calls=%fused_computation.4.clone.1 | convolution fusion | flops 205915136 | bytes 659457 | tf_op jit(solution)/shard_map/while/body/eval_jaxpr/dot_general | solution.py:71
  298.8 1.5 dynamic-slice_multiply_fusion.6
  301.7 8.1 %fusion.154 = f32[4,128]{1,0:T(4,128)S(1)} fusion(s32[32768]{0:T(1024)S(1)} %bitcast.48, f32[1,32768]{1,0:T(1,128)S(1)} %get-tuple-element.145, f32[1,32768]{1,0:T(1,128)S(1)} %get-tuple-element.146, f32[1,32768]{1,0:T(1,128)S(1)} %get-tuple-element.147, f32[1,32768]{1,0:T(1,128)S(1)} %get-tuple-element.148, f32[4,128]{1,0:T(4,128)S(1)} %get-tuple-element.157, ...), kind=kOutput, calls=%fused_computation.4.clone.1 | convolution fusion | flops 205915136 | bytes 659457 | tf_op jit(solution)/shard_map/while/body/eval_jaxpr/dot_general | solution.py:71
  309.8 1.5 dynamic-slice_multiply_fusion.6
  312.6 8.1 %fusion.154 = f32[4,128]{1,0:T(4,128)S(1)} fusion(s32[32768]{0:T(1024)S(1)} %bitcast.48, f32[1,32768]{1,0:T(1,128)S(1)} %get-tuple-element.145, f32[1,32768]{1,0:T(1,128)S(1)} %get-tuple-element.146, f32[1,32768]{1,0:T(1,128)S(1)} %get-tuple-element.147, f32[1,32768]{1,0:T(1,128)S(1)} %get-tuple-element.148, f32[4,128]{1,0:T(4,128)S(1)} %get-tuple-element.157, ...), kind=kOutput, calls=%fused_computation.4.clone.1 | convolution fusion | flops 205915136 | bytes 659457 | tf_op jit(solution)/shard_map/while/body/eval_jaxpr/dot_general | solution.py:71
  320.7 1.5 dynamic-slice_multiply_fusion.6
  323.6 8.1 %fusion.154 = f32[4,128]{1,0:T(4,128)S(1)} fusion(s32[32768]{0:T(1024)S(1)} %bitcast.48, f32[1,32768]{1,0:T(1,128)S(1)} %get-tuple-element.145, f32[1,32768]{1,0:T(1,128)S(1)} %get-tuple-element.146, f32[1,32768]{1,0:T(1,128)S(1)} %get-tuple-element.147, f32[1,32768]{1,0:T(1,128)S(1)} %get-tuple-element.148, f32[4,128]{1,0:T(4,128)S(1)} %get-tuple-element.157, ...), kind=kOutput, calls=%fused_computation.4.clone.1 | convolution fusion | flops 205915136 | bytes 659457 | tf_op jit(solution)/shard_map/while/body/eval_jaxpr/dot_general | solution.py:71
  331.7 1.5 dynamic-slice_multiply_fusion.6
  334.5 8.1 %fusion.154 = f32[4,128]{1,0:T(4,128)S(1)} fusion(s32[32768]{0:T(1024)S(1)} %bitcast.48, f32[1,32768]{1,0:T(1,128)S(1)} %get-tuple-element.145, f32[1,32768]{1,0:T(1,128)S(1)} %get-tuple-element.146, f32[1,32768]{1,0:T(1,128)S(1)} %get-tuple-element.147, f32[1,32768]{1,0:T(1,128)S(1)} %get-tuple-element.148, f32[4,128]{1,0:T(4,128)S(1)} %get-tuple-element.157, ...), kind=kOutput, calls=%fused_computation.4.clone.1 | convolution fusion | flops 205915136 | bytes 659457 | tf_op jit(solution)/shard_map/while/body/eval_jaxpr/dot_general | solution.py:71
  342.6 41.4 %psum.23 = f32[4,128]{1,0:T(4,128)S(1)} all-reduce(f32[4,128]{1,0:T(4,128)S(1)} %get-tuple-element.34), channel_id=1, replica_groups=mesh['row'=4,'col'=8] {'row','col'}, use_global_device_ids=true, to_apply=%region_7.8 | all-reduce | flops 512 | bytes 4096 | tf_op jit(solution)/shard_map/psum | solution.py:83
  (35 shorter events, 19.9 us)
Async XLA Ops:
  70.9 27.2 %collective-permute-start = (f32[2,16,32,256]{3,2,1,0:T(8,128)S(1)}, f32[2,16,32,256]{3,2,1,0:T(8,128)S(1)}, u32[]{:S(2)}, u32[]{:S(2)}) collective-permute-start(f32[2,16,32,256]{3,2,1,0:T(8,128)S(1)} %get-tuple-element.75), channel_id=1, source_target_pairs={{0,8},{8,16},{16,24},{1,9},{9,17},{17,25},{2,10},{10,18},{18,26},{... | collective-permute-start | bytes 3145736 | tf_op jit(solution)/shard_map/ppermute | solution.py:17
  75.9 46.8 %collective-permute-start.1 = (f32[2,16,32,256]{3,2,1,0:T(8,128)S(1)}, f32[2,16,32,256]{3,2,1,0:T(8,128)S(1)}, u32[]{:S(2)}, u32[]{:S(2)}) collective-permute-start(f32[2,16,32,256]{3,2,1,0:T(8,128)S(1)} %get-tuple-element.76), channel_id=1, source_target_pairs={{8,0},{16,8},{24,16},{9,1},{17,9},{25,17},{10,2},{18,10},{26,18},{... | collective-permute-start | bytes 3145736 | tf_op jit(solution)/shard_map/ppermute | solution.py:18
  98.2 25.1 %copy-start.4 = (f32[2,16,32,256]{3,2,1,0:T(8,128)}, f32[2,16,32,256]{3,2,1,0:T(8,128)S(1)}, u32[]{:S(2)}) copy-start(f32[2,16,32,256]{3,2,1,0:T(8,128)S(1)} %collective-permute-done) | copy-start | bytes 3145732
  122.6 1.1 copy-start.5
  123.7 6.3 %copy-start = (s32[32,32,256]{2,1,0:T(8,128)S(1)}, s32[32,32,256]{2,1,0:T(8,128)}, u32[]{:S(2)}) copy-start(s32[32,32,256]{2,1,0:T(8,128)} %param.8) | copy-start | bytes 3145732
  123.7 6.3 %copy-start.2 = (f32[32,32,256]{2,1,0:T(8,128)S(1)}, f32[32,32,256]{2,1,0:T(8,128)}, u32[]{:S(2)}) copy-start(f32[32,32,256]{2,1,0:T(8,128)} %param.7) | copy-start | bytes 3145732
  123.7 6.3 %copy-start.3 = (f32[32,32,256]{2,1,0:T(8,128)S(1)}, f32[32,32,256]{2,1,0:T(8,128)}, u32[]{:S(2)}) copy-start(f32[32,32,256]{2,1,0:T(8,128)} %param.6) | copy-start | bytes 3145732
  126.1 58.9 %collective-permute-start.2 = (f32[2,64,16,256]{3,2,1,0:T(8,128)}, f32[2,64,16,256]{3,2,1,0:T(8,128)}, u32[]{:S(2)}, u32[]{:S(2)}) collective-permute-start(f32[2,64,16,256]{3,2,1,0:T(8,128)} %get-tuple-element.73), channel_id=1, source_target_pairs={{0,1},{1,2},{2,3},{3,4},{4,5},{5,6},{6,7},{8,9},{9,10},{10,11},{11... | collective-permute-start | bytes 6291464 | tf_op jit(solution)/shard_map/ppermute | solution.py:17
  128.7 56.3 %collective-permute-start.3 = (f32[2,64,16,256]{3,2,1,0:T(8,128)}, f32[2,64,16,256]{3,2,1,0:T(8,128)}, u32[]{:S(2)}, u32[]{:S(2)}) collective-permute-start(f32[2,64,16,256]{3,2,1,0:T(8,128)} %get-tuple-element.74), channel_id=1, source_target_pairs={{1,0},{2,1},{3,2},{4,3},{5,4},{6,5},{7,6},{9,8},{10,9},{11,10},{12... | collective-permute-start | bytes 6291464 | tf_op jit(solution)/shard_map/ppermute | solution.py:18
  254.0 1.0 copy-start.1
where the time goes:
time: 387 us; the launch traced here: 385 us
  other arithmetic  153 us (40%)
  blocking collectives  88 us (23%)
  matrix products  64.8 us (17%)
  waiting for transfers between devices  45.5 us (12%)
  local copies, waits for them, and re-layouts  20.9 us (5%)
  starting transfers between devices  10.1 us (3%)
    add x3, other arithmetic, valid_taps(): total = total + taps[j] * lax.slice_in_dim(padded, j, j + count, axis=axis)  130 us
    dot_general x8, matrix products, accumulate(): lax.dot_general(powers, onehot, (((1,), (1,)), ((), ())), precision=lax.P...  64.8 us
    psum x1, blocking collectives, local(): lax.psum((jnp.sum(cover * galaxy), jnp.sum(cover * randoms)), ('row', 'co...  46.6 us
    psum x1, blocking collectives, local(): whole_sums = lax.psum(local_sums, ('row', 'col'))  41.4 us
    ppermute x2, waiting for transfers between devices, extended_2(): after = lax.ppermute(first, axis, down)  24.4 us
    ppermute x2, waiting for transfers between devices, extended_2(): before = lax.ppermute(last, axis, up)  21 us
    mul x8, other arithmetic, accumulate(): mvals * cvals * cvals * cvals  12 us
    dynamic_slice x8, local copies, waits for them, and re-layouts, local(): lax.scan(accumulate, jnp.zeros((4, NPATCH), jnp.float32), (flat_c, flat_m...  10.6 us
  transfers between devices with their start and end apart: 4, of which 2 were waited for; matrix products, arithmetic and copies ran while one was open for 2% of the time, Pallas kernels for 0%

commit v1 on v0

--- a/solution.py
+++ b/solution.py
@@ -42,7 +42,7 @@
     widths = ((0, 0), (0, 0), (0, 0), (radius, radius))
     zsmooth = valid_taps(jnp.pad(fields, widths), taps, radius, 3)
     cover = coverage.astype(jnp.float32)
-    totals = lax.psum((jnp.sum(cover * galaxy), jnp.sum(cover * randoms)), ("row", "col"))
+    totals = lax.psum(lax.psum((jnp.sum(cover * galaxy), jnp.sum(cover * randoms)), "col"), "row")
     extended = extended_2(zsmooth, (("row", 1), ("col", 2)), radius)
     xsmooth = valid_taps(extended, taps, radius, 1)
     smoothed = valid_taps(xsmooth, taps, radius, 2)

time: 387 us -> 379 us (0.979)
  blocking collectives: 88 us -> 81.9 us
    psum x1 -> x2, blocking collectives: 46.6 us -> 43.8 us  [the longest x1 34 us: local(): lax.psum((jnp.sum(cover * galaxy), jnp.sum(cover * randoms)), 'col')]
where the time goes in v1:
time: 379 us; the launch traced here: 377 us
  other arithmetic  152 us (40%)
  blocking collectives  81.9 us (22%)
  matrix products  64.8 us (17%)
  waiting for transfers between devices  45.5 us (12%)
  local copies, waits for them, and re-layouts  20.9 us (6%)
  starting transfers between devices  10.1 us (3%)
    add x3, other arithmetic, valid_taps(): total = total + taps[j] * lax.slice_in_dim(padded, j, j + count, axis=axis)  129 us
    dot_general x8, matrix products, accumulate(): lax.dot_general(powers, onehot, (((1,), (1,)), ((), ())), precision=lax.P...  64.8 us
    psum x1, blocking collectives, local(): whole_sums = lax.psum(local_sums, ('row', 'col'))  38.1 us
    psum x1, blocking collectives, local(): lax.psum((jnp.sum(cover * galaxy), jnp.sum(cover * randoms)), 'col')  34 us
    ppermute x2, waiting for transfers between devices, extended_2(): after = lax.ppermute(first, axis, down)  24.4 us
    ppermute x2, waiting for transfers between devices, extended_2(): before = lax.ppermute(last, axis, up)  21 us
    mul x8, other arithmetic, accumulate(): mvals * cvals * cvals * cvals  12 us
    dynamic_slice x8, local copies, waits for them, and re-layouts, local(): lax.scan(accumulate, jnp.zeros((4, NPATCH), jnp.float32), (flat_c, flat_m...  10.6 us
  transfers between devices with their start and end apart: 4, of which 2 were waited for; matrix products, arithmetic and copies ran while one was open for 2% of the time, Pallas kernels for 0%

profile of v1, /device:TPU:0, one launch (start us, length us, event | category | flops | bytes accessed | tf_op | source)
XLA Modules:
  0.0 377.4 jit_solution(1434159690589398422)
XLA Ops:
  3.4 3.1 pad_maximum_fusion.2
  6.5 63.3 %fusion.99 = f32[2,32,32,256]{3,2,1,0:T(8,128)S(1)} fusion(f32[2,32,32,256]{3,2,1,0:T(8,128)} %pad_maximum_fusion.2, f32[]{:T(128)} %bitcast.34, f32[]{:T(128)} %bitcast.33, f32[]{:T(128)} %bitcast.32, f32[]{:T(128)} %bitcast.31, f32[]{:T(128)} %bitcast.30, f32[]{:T(128)} %bitcast.29, f32[]{:T(128)} %bitcast.28, f32[]{:T(128)} %bitcast.27, f32[]{:T(128)} %bitcast.26, ...), kind=kLoop, calls=%fused_computation.171 | loop fusion | flops 34078720 | bytes 4194436 | tf_op jit(solution)/shard_map/add | solution.py:34
  70.1 4.9 %collective-permute-start = (f32[2,16,32,256]{3,2,1,0:T(8,128)S(1)}, f32[2,16,32,256]{3,2,1,0:T(8,128)S(1)}, u32[]{:S(2)}, u32[]{:S(2)}) collective-permute-start(f32[2,16,32,256]{3,2,1,0:T(8,128)S(1)} %get-tuple-element.77), channel_id=1, source_target_pairs={{0,8},{8,16},{16,24},{1,9},{9,17},{17,25},{2,10},{10,18},{18,26},{... | collective-permute-start | bytes 3145736 | tf_op jit(solution)/shard_map/ppermute | solution.py:17
  76.3 21.0 %collective-permute-done = f32[2,16,32,256]{3,2,1,0:T(8,128)S(1)} collective-permute-done((f32[2,16,32,256]{3,2,1,0:T(8,128)S(1)}, f32[2,16,32,256]{3,2,1,0:T(8,128)S(1)}, u32[]{:S(2)}, u32[]{:S(2)}) %collective-permute-start) | collective-permute-done | bytes 1048608 | tf_op jit(solution)/shard_map/ppermute | solution.py:17
  97.3 24.4 %collective-permute-done.1 = f32[2,16,32,256]{3,2,1,0:T(8,128)S(1)} collective-permute-done((f32[2,16,32,256]{3,2,1,0:T(8,128)S(1)}, f32[2,16,32,256]{3,2,1,0:T(8,128)S(1)}, u32[]{:S(2)}, u32[]{:S(2)}) %collective-permute-start.1) | collective-permute-done | bytes 1048608 | tf_op jit(solution)/shard_map/ppermute | solution.py:18
  122.8 2.4 fusion.147
  125.2 2.6 collective-permute-start.2
  130.2 34.0 %all-reduce.1 = (f32[]{:T(128)}, f32[]{:T(128)}) all-reduce(f32[]{:T(128)} %get-tuple-element.56, f32[]{:T(128)} %get-tuple-element.55), channel_id=1, replica_groups=mesh['row'=4,'col'=8] {'col'}, use_global_device_ids=true, to_apply=%region_1.2 | all-reduce | flops 2 | bytes 16 | tf_op jit(solution)/shard_map/psum | solution.py:45
  164.3 9.8 %all-reduce.2 = (f32[]{:T(128)}, f32[]{:T(128)}) all-reduce(f32[]{:T(128)} %get-tuple-element.67, f32[]{:T(128)} %get-tuple-element.68), channel_id=1, replica_groups=mesh['row'=4,'col'=8] {'row'}, use_global_device_ids=true, to_apply=%region_2.3 | all-reduce | flops 2 | bytes 16 | tf_op jit(solution)/shard_map/psum | solution.py:45
  175.1 2.5 reshape.25
  177.5 2.4 reshape.27
  181.2 3.3 pad_maximum_fusion
  184.4 36.4 %fusion.13 = f32[2,32,64,256]{3,2,1,0:T(8,128)S(1)} fusion(f32[2,64,64,256]{3,2,1,0:T(8,128)S(1)} %pad_maximum_fusion, f32[]{:T(128)} %bitcast.34, f32[]{:T(128)} %bitcast.33, f32[]{:T(128)} %bitcast.32, f32[]{:T(128)} %bitcast.31, f32[]{:T(128)} %bitcast.30, f32[]{:T(128)} %bitcast.29, f32[]{:T(128)} %bitcast.28, f32[]{:T(128)} %bitcast.27, f32[]{:T(128)} %bitcast.26, ...), kind=kLoop, calls=%fused_computation.52 | loop fusion | flops 68157440 | bytes 142606464 | tf_op jit(solution)/shard_map/add | solution.py:34
  220.8 28.9 %fusion.109 = f32[2,32,32,256]{3,2,1,0:T(8,128)S(1)} fusion(f32[2,32,64,256]{3,2,1,0:T(8,128)S(1)} %fusion.13, f32[]{:T(128)} %bitcast.34, f32[]{:T(128)} %bitcast.33, f32[]{:T(128)} %bitcast.32, f32[]{:T(128)} %bitcast.31, f32[]{:T(128)} %bitcast.30, f32[]{:T(128)} %bitcast.29, f32[]{:T(128)} %bitcast.28, f32[]{:T(128)} %bitcast.27, f32[]{:T(128)} %bitcast.26, ...), kind=kLoop, calls=%fused_computation.182 | loop fusion | flops 34078720 | bytes 71303296 | tf_op jit(solution)/shard_map/add | solution.py:34
  251.1 87.6 %while.11 = (s32[]{:T(128)}, f32[4,128]{1,0:T(4,128)S(1)}, f32[8,32768]{1,0:T(8,128)}, f32[8,32768]{1,0:T(8,128)S(1)}, s32[8,32768]{1,0:T(8,128)}, /*index=5*/s32[]{:T(128)}, s32[]{:T(128)}) while((s32[]{:T(128)}, f32[4,128]{1,0:T(4,128)S(1)}, f32[8,32768]{1,0:T(8,128)}, f32[8,32768]{1,0:T(8,128)S(1)}, s32[8,32768]{1,0:T(8,128)}, ...), condition=%wide.region_8.9_spmd.clone, body=%wide.region_7.8_spmd.clone.sunk | while | flops 206013440 | bytes 1708127 | solution.py:80
  251.1 1.5 dynamic-slice_multiply_fusion.6
  253.9 8.1 %fusion.154 = f32[4,128]{1,0:T(4,128)S(1)} fusion(s32[32768]{0:T(1024)S(1)} %bitcast.48, f32[1,32768]{1,0:T(1,128)S(1)} %get-tuple-element.147, f32[1,32768]{1,0:T(1,128)S(1)} %get-tuple-element.148, f32[1,32768]{1,0:T(1,128)S(1)} %get-tuple-element.149, f32[1,32768]{1,0:T(1,128)S(1)} %get-tuple-element.150, f32[4,128]{1,0:T(4,128)S(1)} %get-tuple-element.159, ...), kind=kOutput, calls=%fused_computation.4.clone.1 | convolution fusion | flops 205915136 | bytes 659457 | tf_op jit(solution)/shard_map/while/body/eval_jaxpr/dot_general | solution.py:71
  262.0 1.5 dynamic-slice_multiply_fusion.6
  264.8 8.1 %fusion.154 = f32[4,128]{1,0:T(4,128)S(1)} fusion(s32[32768]{0:T(1024)S(1)} %bitcast.48, f32[1,32768]{1,0:T(1,128)S(1)} %get-tuple-element.147, f32[1,32768]{1,0:T(1,128)S(1)} %get-tuple-element.148, f32[1,32768]{1,0:T(1,128)S(1)} %get-tuple-element.149, f32[1,32768]{1,0:T(1,128)S(1)} %get-tuple-element.150, f32[4,128]{1,0:T(4,128)S(1)} %get-tuple-element.159, ...), kind=kOutput, calls=%fused_computation.4.clone.1 | convolution fusion | flops 205915136 | bytes 659457 | tf_op jit(solution)/shard_map/while/body/eval_jaxpr/dot_general | solution.py:71
  273.0 1.5 dynamic-slice_multiply_fusion.6
  275.8 8.1 %fusion.154 = f32[4,128]{1,0:T(4,128)S(1)} fusion(s32[32768]{0:T(1024)S(1)} %bitcast.48, f32[1,32768]{1,0:T(1,128)S(1)} %get-tuple-element.147, f32[1,32768]{1,0:T(1,128)S(1)} %get-tuple-element.148, f32[1,32768]{1,0:T(1,128)S(1)} %get-tuple-element.149, f32[1,32768]{1,0:T(1,128)S(1)} %get-tuple-element.150, f32[4,128]{1,0:T(4,128)S(1)} %get-tuple-element.159, ...), kind=kOutput, calls=%fused_computation.4.clone.1 | convolution fusion | flops 205915136 | bytes 659457 | tf_op jit(solution)/shard_map/while/body/eval_jaxpr/dot_general | solution.py:71
  283.9 1.5 dynamic-slice_multiply_fusion.6
  286.8 8.1 %fusion.154 = f32[4,128]{1,0:T(4,128)S(1)} fusion(s32[32768]{0:T(1024)S(1)} %bitcast.48, f32[1,32768]{1,0:T(1,128)S(1)} %get-tuple-element.147, f32[1,32768]{1,0:T(1,128)S(1)} %get-tuple-element.148, f32[1,32768]{1,0:T(1,128)S(1)} %get-tuple-element.149, f32[1,32768]{1,0:T(1,128)S(1)} %get-tuple-element.150, f32[4,128]{1,0:T(4,128)S(1)} %get-tuple-element.159, ...), kind=kOutput, calls=%fused_computation.4.clone.1 | convolution fusion | flops 205915136 | bytes 659457 | tf_op jit(solution)/shard_map/while/body/eval_jaxpr/dot_general | solution.py:71
  294.9 1.5 dynamic-slice_multiply_fusion.6
  297.7 8.1 %fusion.154 = f32[4,128]{1,0:T(4,128)S(1)} fusion(s32[32768]{0:T(1024)S(1)} %bitcast.48, f32[1,32768]{1,0:T(1,128)S(1)} %get-tuple-element.147, f32[1,32768]{1,0:T(1,128)S(1)} %get-tuple-element.148, f32[1,32768]{1,0:T(1,128)S(1)} %get-tuple-element.149, f32[1,32768]{1,0:T(1,128)S(1)} %get-tuple-element.150, f32[4,128]{1,0:T(4,128)S(1)} %get-tuple-element.159, ...), kind=kOutput, calls=%fused_computation.4.clone.1 | convolution fusion | flops 205915136 | bytes 659457 | tf_op jit(solution)/shard_map/while/body/eval_jaxpr/dot_general | solution.py:71
  305.8 1.5 dynamic-slice_multiply_fusion.6
  308.7 8.1 %fusion.154 = f32[4,128]{1,0:T(4,128)S(1)} fusion(s32[32768]{0:T(1024)S(1)} %bitcast.48, f32[1,32768]{1,0:T(1,128)S(1)} %get-tuple-element.147, f32[1,32768]{1,0:T(1,128)S(1)} %get-tuple-element.148, f32[1,32768]{1,0:T(1,128)S(1)} %get-tuple-element.149, f32[1,32768]{1,0:T(1,128)S(1)} %get-tuple-element.150, f32[4,128]{1,0:T(4,128)S(1)} %get-tuple-element.159, ...), kind=kOutput, calls=%fused_computation.4.clone.1 | convolution fusion | flops 205915136 | bytes 659457 | tf_op jit(solution)/shard_map/while/body/eval_jaxpr/dot_general | solution.py:71
  316.8 1.5 dynamic-slice_multiply_fusion.6
  319.6 8.1 %fusion.154 = f32[4,128]{1,0:T(4,128)S(1)} fusion(s32[32768]{0:T(1024)S(1)} %bitcast.48, f32[1,32768]{1,0:T(1,128)S(1)} %get-tuple-element.147, f32[1,32768]{1,0:T(1,128)S(1)} %get-tuple-element.148, f32[1,32768]{1,0:T(1,128)S(1)} %get-tuple-element.149, f32[1,32768]{1,0:T(1,128)S(1)} %get-tuple-element.150, f32[4,128]{1,0:T(4,128)S(1)} %get-tuple-element.159, ...), kind=kOutput, calls=%fused_computation.4.clone.1 | convolution fusion | flops 205915136 | bytes 659457 | tf_op jit(solution)/shard_map/while/body/eval_jaxpr/dot_general | solution.py:71
  327.7 1.5 dynamic-slice_multiply_fusion.6
  330.6 8.1 %fusion.154 = f32[4,128]{1,0:T(4,128)S(1)} fusion(s32[32768]{0:T(1024)S(1)} %bitcast.48, f32[1,32768]{1,0:T(1,128)S(1)} %get-tuple-element.147, f32[1,32768]{1,0:T(1,128)S(1)} %get-tuple-element.148, f32[1,32768]{1,0:T(1,128)S(1)} %get-tuple-element.149, f32[1,32768]{1,0:T(1,128)S(1)} %get-tuple-element.150, f32[4,128]{1,0:T(4,128)S(1)} %get-tuple-element.159, ...), kind=kOutput, calls=%fused_computation.4.clone.1 | convolution fusion | flops 205915136 | bytes 659457 | tf_op jit(solution)/shard_map/while/body/eval_jaxpr/dot_general | solution.py:71
  338.7 38.1 %psum.39 = f32[4,128]{1,0:T(4,128)S(1)} all-reduce(f32[4,128]{1,0:T(4,128)S(1)} %get-tuple-element.34), channel_id=1, replica_groups=mesh['row'=4,'col'=8] {'row','col'}, use_global_device_ids=true, to_apply=%region_9.10 | all-reduce | flops 512 | bytes 4096 | tf_op jit(solution)/shard_map/psum | solution.py:83
  (36 shorter events, 21.2 us)
Async XLA Ops:
  70.1 27.2 %collective-permute-start = (f32[2,16,32,256]{3,2,1,0:T(8,128)S(1)}, f32[2,16,32,256]{3,2,1,0:T(8,128)S(1)}, u32[]{:S(2)}, u32[]{:S(2)}) collective-permute-start(f32[2,16,32,256]{3,2,1,0:T(8,128)S(1)} %get-tuple-element.77), channel_id=1, source_target_pairs={{0,8},{8,16},{16,24},{1,9},{9,17},{17,25},{2,10},{10,18},{18,26},{... | collective-permute-start | bytes 3145736 | tf_op jit(solution)/shard_map/ppermute | solution.py:17
  75.0 46.8 %collective-permute-start.1 = (f32[2,16,32,256]{3,2,1,0:T(8,128)S(1)}, f32[2,16,32,256]{3,2,1,0:T(8,128)S(1)}, u32[]{:S(2)}, u32[]{:S(2)}) collective-permute-start(f32[2,16,32,256]{3,2,1,0:T(8,128)S(1)} %get-tuple-element.78), channel_id=1, source_target_pairs={{8,0},{16,8},{24,16},{9,1},{17,9},{25,17},{10,2},{18,10},{26,18},{... | collective-permute-start | bytes 3145736 | tf_op jit(solution)/shard_map/ppermute | solution.py:18
  97.3 25.1 %copy-start.4 = (f32[2,16,32,256]{3,2,1,0:T(8,128)}, f32[2,16,32,256]{3,2,1,0:T(8,128)S(1)}, u32[]{:S(2)}) copy-start(f32[2,16,32,256]{3,2,1,0:T(8,128)S(1)} %collective-permute-done) | copy-start | bytes 3145732
  121.7 1.1 copy-start.5
  122.8 6.3 %copy-start = (s32[32,32,256]{2,1,0:T(8,128)S(1)}, s32[32,32,256]{2,1,0:T(8,128)}, u32[]{:S(2)}) copy-start(s32[32,32,256]{2,1,0:T(8,128)} %param.8) | copy-start | bytes 3145732
  122.8 6.3 %copy-start.2 = (f32[32,32,256]{2,1,0:T(8,128)S(1)}, f32[32,32,256]{2,1,0:T(8,128)}, u32[]{:S(2)}) copy-start(f32[32,32,256]{2,1,0:T(8,128)} %param.7) | copy-start | bytes 3145732
  122.8 6.3 %copy-start.3 = (f32[32,32,256]{2,1,0:T(8,128)S(1)}, f32[32,32,256]{2,1,0:T(8,128)}, u32[]{:S(2)}) copy-start(f32[32,32,256]{2,1,0:T(8,128)} %param.6) | copy-start | bytes 3145732
  125.2 55.9 %collective-permute-start.2 = (f32[2,64,16,256]{3,2,1,0:T(8,128)}, f32[2,64,16,256]{3,2,1,0:T(8,128)}, u32[]{:S(2)}, u32[]{:S(2)}) collective-permute-start(f32[2,64,16,256]{3,2,1,0:T(8,128)} %get-tuple-element.75), channel_id=1, source_target_pairs={{0,1},{1,2},{2,3},{3,4},{4,5},{5,6},{6,7},{8,9},{9,10},{10,11},{11... | collective-permute-start | bytes 6291464 | tf_op jit(solution)/shard_map/ppermute | solution.py:17
  127.8 53.3 %collective-permute-start.3 = (f32[2,64,16,256]{3,2,1,0:T(8,128)}, f32[2,64,16,256]{3,2,1,0:T(8,128)}, u32[]{:S(2)}, u32[]{:S(2)}) collective-permute-start(f32[2,64,16,256]{3,2,1,0:T(8,128)} %get-tuple-element.76), channel_id=1, source_target_pairs={{1,0},{2,1},{3,2},{4,3},{5,4},{6,5},{7,6},{9,8},{10,9},{11,10},{12... | collective-permute-start | bytes 6291464 | tf_op jit(solution)/shard_map/ppermute | solution.py:18
  250.1 1.0 copy-start.1
